TPU v7x, 32 devices: a whole 2x2x4 slice. The times are simulated.
32 devices in a mesh: fsdp: 4 (over y, core), ctx: 8 (over z, x).
Axes of the slice: x: 2, y: 2, z: 4, core: 2. Of those that a mesh axis runs over, the one named last changes fastest.
Arguments:
- block_input: bfloat16 [4, 1024, 1024], P('fsdp', 'ctx'), may hold values from -12 to 12
- positions: int32 [4, 1024], P('fsdp', 'ctx'), may hold values from 0 to 999, as said below
- attn_norm_gain: bfloat16 [1024], replicated, may hold values from 0.099609375 to 1.8984375
- w_query: bfloat16 [1024, 2048], P('fsdp'), may hold values from -0.1875 to 0.1875
- key_projection: bfloat16 [1024, 1024], P('fsdp'), may hold values from -0.1875 to 0.1875
- value_projection: bfloat16 [1024, 1024], P('fsdp'), may hold values from -0.1875 to 0.1875
- query_norm_gain: bfloat16 [128], replicated, may hold values from 0.5 to 2
- key_norm_gain: bfloat16 [128], replicated, may hold values from 0.5 to 2
- output_projection: bfloat16 [2048, 1024], P('fsdp'), may hold values from -0.75 to 0.75
- ffn_norm_gain: bfloat16 [1024], replicated, may hold values from 0.099609375 to 1.8984375
- w_gate: bfloat16 [1024, 3072], P('fsdp'), may hold values from -0.1875 to 0.1875
- w_up: bfloat16 [1024, 3072], P('fsdp'), may hold values from -0.1875 to 0.1875
- w_down: bfloat16 [3072, 1024], P('fsdp'), may hold values from -0.109375 to 0.109375
- out_cotangent: bfloat16 [4, 1024, 1024], P('fsdp', 'ctx'), may hold values from -6 to 6
Outputs:
- block_output: bfloat16 [4, 1024, 1024], P('fsdp', 'ctx')
- input_grad: float32 [4, 1024, 1024], P('fsdp', 'ctx')
- attn_gain_grad: float32 [1024], replicated
- query_weight_grad: float32 [1024, 2048], P('fsdp')
- key_weight_grad: float32 [1024, 1024], P('fsdp')
- value_weight_grad: float32 [1024, 1024], P('fsdp')
- query_gain_grad: float32 [128], replicated
- key_gain_grad: float32 [128], replicated
- output_weight_grad: float32 [2048, 1024], P('fsdp')
- ffn_gain_grad: float32 [1024], replicated
- gate_weight_grad: float32 [1024, 3072], P('fsdp')
- up_weight_grad: float32 [1024, 3072], P('fsdp')
- down_weight_grad: float32 [3072, 1024], P('fsdp')
Inputs may be any that keep to these rules, and one draw needn't show every extreme that they name: Each sequence is a run of documents: positions count 0, 1, 2, ... within a document and restart at 0 where a new one begins. Every document has at most 1000 tokens and the longest has exactly 1000; all but a sequence's last have at least 102.
All inputs are finite; a program needn't handle non-finite values.
Results may differ from a plain program's by a relative error of at most 0.02.
Values may be sent and summed in bfloat16 or wider, within the bound.
A program may use at most 320 MiB of HBM per device.

v0:
```python
import math

import jax
import jax.numpy as jnp
from jax import lax
from jax.sharding import PartitionSpec as P

QUERY_HEADS = 16
KEY_VALUE_HEADS = 8
HEAD_SIZE = 128
FF = 3072


EPSILON = 1e-06
ROPE_BASE = 1000000.0
MASK_FLOOR = -1e30


def inverse_rms(values):
    return lax.rsqrt(jnp.mean(values * values, axis=-1, keepdims=True) + EPSILON)


def norm_reverse(grad_out, values, inv_scale, gain_vector):
    gained = gain_vector * grad_out
    cubed = inv_scale * inv_scale * inv_scale
    return inv_scale * gained - values * cubed * jnp.mean(gained * values, axis=-1, keepdims=True)


def rope_tables(places):
    half_dim = HEAD_SIZE // 2
    frequency = ROPE_BASE ** (-(jnp.arange(half_dim, dtype=jnp.float32) * 2.0 / HEAD_SIZE))
    angles = places.astype(jnp.float32)[:, None] * frequency[None, :]
    return (jnp.cos(angles)[:, None, :], jnp.sin(angles)[:, None, :])


def apply_rotary(values, cosine_lookup, sine_lookup):
    half_dim = HEAD_SIZE // 2
    first_half = values[..., :half_dim]
    second_half = values[..., half_dim:]
    return jnp.concatenate(
        [
            first_half * cosine_lookup - second_half * sine_lookup,
            second_half * cosine_lookup + first_half * sine_lookup,
        ],
        axis=-1,
    )


def reverse_rotary(grad_in, cosine_lookup, sine_lookup):
    half_dim = HEAD_SIZE // 2
    first_half = grad_in[..., :half_dim]
    second_half = grad_in[..., half_dim:]
    return jnp.concatenate(
        [
            first_half * cosine_lookup + second_half * sine_lookup,
            second_half * cosine_lookup - first_half * sine_lookup,
        ],
        axis=-1,
    )


def contract_rows(left, right):
    return lax.dot_general(
        left, right, (((0,), (0,)), ((), ())), preferred_element_type=jnp.float32
    )


def times_transpose(left, right):
    return lax.dot_general(
        left, right, (((1,), (1,)), ((), ())), preferred_element_type=jnp.float32
    )


def sum_blocks(row_shares):
    flat_terms = tuple((matrix.reshape(-1) for matrix in row_shares))
    pieces = lax.psum_scatter(flat_terms, "ctx", scatter_dimension=0, tiled=True)
    whole_rows = lax.all_gather(pieces, "ctx", axis=0, tiled=True)
    return tuple(
        (summed_part.reshape(matrix.shape) for summed_part, matrix in zip(whole_rows, row_shares))
    )


def local(
    block_input,
    positions,
    attn_norm_gain,
    w_query,
    key_projection,
    value_projection,
    query_norm_gain,
    key_norm_gain,
    output_projection,
    ffn_norm_gain,
    w_gate,
    w_up,
    w_down,
    out_cotangent,
):
    full_query, complete_key, full_value, full_output, full_gate, full_up, full_down = (
        lax.all_gather(w_query, "fsdp", axis=0, tiled=True),
        lax.all_gather(key_projection, "fsdp", axis=0, tiled=True),
        lax.all_gather(value_projection, "fsdp", axis=0, tiled=True),
        lax.all_gather(output_projection, "fsdp", axis=0, tiled=True),
        lax.all_gather(w_gate, "fsdp", axis=0, tiled=True),
        lax.all_gather(w_up, "fsdp", axis=0, tiled=True),
        lax.all_gather(w_down, "fsdp", axis=0, tiled=True),
    )
    token_count = block_input.shape[1]
    sequence_length = token_count * lax.axis_size("ctx")
    query_groups = QUERY_HEADS // KEY_VALUE_HEADS
    query_width = QUERY_HEADS * HEAD_SIZE
    group_width = KEY_VALUE_HEADS * HEAD_SIZE
    key_window = min(512, sequence_length)
    scale_factor = 1.0 / math.sqrt(HEAD_SIZE)
    inputs = block_input[0].astype(jnp.float32)
    places = positions[0]
    first_row = lax.axis_index("ctx") * token_count
    row_ids = first_row + jnp.arange(token_count, dtype=jnp.int32)
    doc_starts = row_ids - places
    gain_one = attn_norm_gain.astype(jnp.float32)
    scale_one = inverse_rms(inputs)
    normalized_input = (inputs * scale_one * gain_one).astype(jnp.bfloat16)
    query_projected = jnp.dot(
        normalized_input, full_query, preferred_element_type=jnp.float32
    ).reshape(token_count, QUERY_HEADS, HEAD_SIZE)
    key_projected = jnp.dot(
        normalized_input, complete_key, preferred_element_type=jnp.float32
    ).reshape(token_count, KEY_VALUE_HEADS, HEAD_SIZE)
    values = jnp.dot(normalized_input, full_value, preferred_element_type=jnp.float32).astype(
        jnp.bfloat16
    )
    query_norm_scale = inverse_rms(query_projected)
    key_norm_scale = inverse_rms(key_projected)
    query_gain_wide32 = query_norm_gain.astype(jnp.float32)
    key_gain_wide32 = key_norm_gain.astype(jnp.float32)
    cosine_lookup, sine_lookup = rope_tables(places)
    query_rot = (
        apply_rotary(
            query_projected * query_norm_scale * query_gain_wide32, cosine_lookup, sine_lookup
        )
        .astype(jnp.bfloat16)
        .reshape(token_count, KEY_VALUE_HEADS, query_groups, HEAD_SIZE)
    )
    key_rot = (
        apply_rotary(key_projected * key_norm_scale * key_gain_wide32, cosine_lookup, sine_lookup)
        .astype(jnp.bfloat16)
        .reshape(token_count, group_width)
    )
    all_keys, all_values = (
        lax.all_gather(key_rot, "ctx", axis=0, tiled=True),
        lax.all_gather(values, "ctx", axis=0, tiled=True),
    )
    lower_block = jnp.min(doc_starts) // key_window
    upper_block = (first_row + token_count - 1) // key_window + 1

    def fetch(block_index):
        token_shift = block_index * key_window
        key_block = lax.dynamic_slice_in_dim(all_keys, token_shift, key_window, 0).reshape(
            key_window, KEY_VALUE_HEADS, HEAD_SIZE
        )
        value_block = lax.dynamic_slice_in_dim(all_values, token_shift, key_window, 0).reshape(
            key_window, KEY_VALUE_HEADS, HEAD_SIZE
        )
        columns = token_shift + jnp.arange(key_window, dtype=jnp.int32)
        allowed = (columns[None, :] <= row_ids[:, None]) & (columns[None, :] >= doc_starts[:, None])
        scores = (
            jnp.einsum("tkgd,skd->kgts", query_rot, key_block, preferred_element_type=jnp.float32)
            * scale_factor
        )
        return (
            jnp.where(allowed, scores, MASK_FLOOR),
            key_block,
            value_block,
            token_shift,
            allowed,
        )

    def running_total(block_index, state_now):
        row_peak, running_sum = state_now
        scores, key_block, value_block, token_shift, allowed = fetch(block_index)
        new_peak = jnp.maximum(row_peak, jnp.max(scores, axis=-1))
        terms = jnp.where(allowed, jnp.exp(scores - new_peak[..., None]), 0.0)
        running_sum = running_sum * jnp.exp(row_peak - new_peak) + jnp.sum(terms, axis=-1)
        return (new_peak, running_sum)

    initial_peak = jnp.full((KEY_VALUE_HEADS, query_groups, token_count), MASK_FLOOR, jnp.float32)
    row_peak, running_sum = lax.fori_loop(
        lower_block, upper_block, running_total, (initial_peak, jnp.zeros_like(initial_peak))
    )
    log_total = row_peak + jnp.log(running_sum)

    def weighted_values(block_index, weighted_sum):
        scores, key_block, value_block, token_shift, allowed = fetch(block_index)
        probability = jnp.exp(scores - log_total[..., None]).astype(jnp.bfloat16)
        return weighted_sum + jnp.einsum(
            "kgts,skd->tkgd", probability, value_block, preferred_element_type=jnp.float32
        )

    weighted_sum = lax.fori_loop(
        lower_block,
        upper_block,
        weighted_values,
        jnp.zeros((token_count, KEY_VALUE_HEADS, query_groups, HEAD_SIZE), jnp.float32),
    )
    attention_output = weighted_sum.reshape(token_count, query_width).astype(jnp.bfloat16)
    middle = inputs + jnp.dot(attention_output, full_output, preferred_element_type=jnp.float32)
    scale_two = inverse_rms(middle)
    gain_two = ffn_norm_gain.astype(jnp.float32)
    normed_two = (middle * scale_two * gain_two).astype(jnp.bfloat16)
    gate_proj = jnp.dot(normed_two, full_gate, preferred_element_type=jnp.float32)
    upper = jnp.dot(normed_two, full_up, preferred_element_type=jnp.float32)
    gate_sigmoid = jax.nn.sigmoid(gate_proj)
    hidden = (gate_proj * gate_sigmoid * upper).astype(jnp.bfloat16)
    result = middle + jnp.dot(hidden, full_down, preferred_element_type=jnp.float32)
    block_output = result.astype(jnp.bfloat16)[None]
    back_query, back_key, back_value = (full_query, complete_key, full_value)
    back_output, back_gate, back_up, back_down = (full_output, full_gate, full_up, full_down)
    cotangent = out_cotangent[0]
    hidden_grad = times_transpose(cotangent, back_down)
    gate_grad = (
        hidden_grad * upper * gate_sigmoid * (1.0 + gate_proj * (1.0 - gate_sigmoid))
    ).astype(jnp.bfloat16)
    up_grad = (hidden_grad * gate_proj * gate_sigmoid).astype(jnp.bfloat16)
    nt_grad = times_transpose(gate_grad, back_gate) + times_transpose(up_grad, back_up)
    ffn_gain_term = jnp.sum(nt_grad * middle * scale_two, axis=0)
    middle_grad = cotangent.astype(jnp.float32) + norm_reverse(nt_grad, middle, scale_two, gain_two)
    middle_narrow = middle_grad.astype(jnp.bfloat16)
    down_rows = lax.psum_scatter(
        contract_rows(hidden, cotangent), "fsdp", scatter_dimension=0, tiled=True
    )
    output_rows = lax.psum_scatter(
        contract_rows(attention_output, middle_narrow), "fsdp", scatter_dimension=0, tiled=True
    )
    attention_gradient = (
        times_transpose(middle_narrow, back_output)
        .astype(jnp.bfloat16)
        .reshape(token_count, KEY_VALUE_HEADS, query_groups, HEAD_SIZE)
    )
    output_product = jnp.sum(
        attention_gradient.astype(jnp.float32)
        * attention_output.astype(jnp.float32).reshape(
            token_count, KEY_VALUE_HEADS, query_groups, HEAD_SIZE
        ),
        axis=-1,
    )
    output_product = jnp.transpose(output_product, (1, 2, 0))

    def back_block(block_index, state_now):
        query_grad, key_contributions, value_contributions = state_now
        scores, key_block, value_block, token_shift, allowed = fetch(block_index)
        probability = jnp.exp(scores - log_total[..., None])
        value_portion = jnp.einsum(
            "kgts,tkgd->skd",
            probability.astype(jnp.bfloat16),
            attention_gradient,
            preferred_element_type=jnp.float32,
        )
        prob_grad = jnp.einsum(
            "tkgd,skd->kgts", attention_gradient, value_block, preferred_element_type=jnp.float32
        )
        score_grad = (probability * (prob_grad - output_product[..., None])).astype(jnp.bfloat16)
        query_grad = (
            query_grad
            + jnp.einsum(
                "kgts,skd->tkgd", score_grad, key_block, preferred_element_type=jnp.float32
            )
            * scale_factor
        )
        key_portion = (
            jnp.einsum("kgts,tkgd->skd", score_grad, query_rot, preferred_element_type=jnp.float32)
            * scale_factor
        )
        key_previous = lax.dynamic_slice_in_dim(key_contributions, token_shift, key_window, 0)
        key_contributions = lax.dynamic_update_slice_in_dim(
            key_contributions,
            key_previous + key_portion.reshape(key_window, group_width),
            token_shift,
            0,
        )
        value_previous = lax.dynamic_slice_in_dim(value_contributions, token_shift, key_window, 0)
        value_contributions = lax.dynamic_update_slice_in_dim(
            value_contributions,
            value_previous + value_portion.reshape(key_window, group_width),
            token_shift,
            0,
        )
        return (query_grad, key_contributions, value_contributions)

    empty_keys = jnp.zeros((sequence_length, group_width), jnp.float32)
    query_grad, key_contributions, value_contributions = lax.fori_loop(
        lower_block,
        upper_block,
        back_block,
        (
            jnp.zeros((token_count, KEY_VALUE_HEADS, query_groups, HEAD_SIZE), jnp.float32),
            empty_keys,
            empty_keys,
        ),
    )
    key_total_sum, value_sum = (
        lax.psum_scatter(
            key_contributions.astype(jnp.bfloat16), "ctx", scatter_dimension=0, tiled=True
        ).astype(jnp.float32),
        lax.psum_scatter(
            value_contributions.astype(jnp.bfloat16), "ctx", scatter_dimension=0, tiled=True
        ).astype(jnp.float32),
    )
    query_pre = reverse_rotary(
        query_grad.reshape(token_count, QUERY_HEADS, HEAD_SIZE), cosine_lookup, sine_lookup
    )
    key_unnormed = reverse_rotary(
        key_total_sum.reshape(token_count, KEY_VALUE_HEADS, HEAD_SIZE), cosine_lookup, sine_lookup
    )
    query_gain_term = jnp.sum(query_pre * query_projected * query_norm_scale, axis=(0, 1))
    key_gain_term = jnp.sum(key_unnormed * key_projected * key_norm_scale, axis=(0, 1))
    query_low = (
        norm_reverse(query_pre, query_projected, query_norm_scale, query_gain_wide32)
        .reshape(token_count, query_width)
        .astype(jnp.bfloat16)
    )
    key_narrow = (
        norm_reverse(key_unnormed, key_projected, key_norm_scale, key_gain_wide32)
        .reshape(token_count, group_width)
        .astype(jnp.bfloat16)
    )
    value_narrow = value_sum.astype(jnp.bfloat16)
    normed_grad = (
        times_transpose(query_low, back_query)
        + times_transpose(key_narrow, back_key)
        + times_transpose(value_narrow, back_value)
    )
    attn_gain_term = jnp.sum(normed_grad * inputs * scale_one, axis=0)
    input_grad = middle_grad + norm_reverse(normed_grad, inputs, scale_one, gain_one)
    attn_side = jnp.concatenate([query_low, key_narrow, value_narrow], axis=1)
    ffn_side = jnp.concatenate([gate_grad, up_grad], axis=1)
    first_part = contract_rows(normalized_input, attn_side)
    second_part = contract_rows(normed_two, ffn_side)
    input_rows = lax.psum_scatter(
        jnp.concatenate([first_part, second_part], axis=1), "fsdp", scatter_dimension=0, tiled=True
    )
    input_sum, output_sum, down_sum = sum_blocks((input_rows, output_rows, down_rows))
    query_sum = input_sum[:, :query_width]
    key_wsum = input_sum[:, query_width : query_width + group_width]
    value_wsum = input_sum[:, query_width + group_width : query_width + 2 * group_width]
    gate_sum = input_sum[:, query_width + 2 * group_width : query_width + 2 * group_width + FF]
    up_sum = input_sum[:, query_width + 2 * group_width + FF :]
    gain_sums = lax.psum(
        (attn_gain_term, query_gain_term, key_gain_term, ffn_gain_term), ("fsdp", "ctx")
    )
    return (
        block_output,
        input_grad[None],
        gain_sums[0],
        query_sum,
        key_wsum,
        value_wsum,
        gain_sums[1],
        gain_sums[2],
        output_sum,
        gain_sums[3],
        gate_sum,
        up_sum,
        down_sum,
    )


def solution(mesh):
    return jax.shard_map(
        local,
        mesh=mesh,
        in_specs=(
            P("fsdp", "ctx", None),
            P("fsdp", "ctx"),
            P(),
            P("fsdp", None),
            P("fsdp", None),
            P("fsdp", None),
            P(),
            P(),
            P("fsdp", None),
            P(),
            P("fsdp", None),
            P("fsdp", None),
            P("fsdp", None),
            P("fsdp", "ctx", None),
        ),
        out_specs=(
            P("fsdp", "ctx", None),
            P("fsdp", "ctx", None),
            P(),
            P("fsdp", None),
            P("fsdp", None),
            P("fsdp", None),
            P(),
            P(),
            P("fsdp", None),
            P(),
            P("fsdp", None),
            P("fsdp", None),
            P("fsdp", None),
        ),
        check_vma=False,
    )
```

profile of v0, /device:TPU:0, one launch (start us, length us, event | category | flops | bytes accessed | tf_op | source)
XLA Modules:
  0.0 1824.6 jit_solution(8952637492006886114)
XLA Ops:
  11.8 23.1 %all-gather.13.cloned.1.call-done = bf16[1024,1024]{1,0:T(8,128)(2,1)} async-done(((bf16[256,1024]{1,0:T(8,128)(2,1)}), bf16[1024,1024]{1,0:T(8,128)(2,1)}) %all-gather.13.cloned.1.call-update) | async-done | bytes 2097168 | tf_op jit(solution)/shard_map/all_gather | solution.py:102
  34.9 2.9 convolution_convert_fusion.1
  38.2 20.9 %all-gather.17.cloned.1.call-done = bf16[1024,1024]{1,0:T(8,128)(2,1)} async-done(((bf16[256,1024]{1,0:T(8,128)(2,1)}), bf16[1024,1024]{1,0:T(8,128)(2,1)}) %all-gather.17.cloned.1.call-update) | async-done | bytes 2097168 | tf_op jit(solution)/shard_map/all_gather | solution.py:101
  59.1 2.9 copy.86
  71.1 24.1 %all-gather.21.cloned.1.call-done = bf16[1024,2048]{1,0:T(8,128)(2,1)} async-done(((bf16[256,2048]{1,0:T(8,128)(2,1)}), bf16[1024,2048]{1,0:T(8,128)(2,1)}) %all-gather.21.cloned.1.call-update) | async-done | bytes 4194320 | tf_op jit(solution)/shard_map/all_gather | solution.py:100
  95.2 6.4 copy.87
  101.6 3.5 multiply_reduce_fusion.3
  106.6 40.5 %all-gather.15.cloned.1.call-done = bf16[1024,1024]{1,0:T(8,128)(2,1)} async-done(((bf16[128,1024]{1,0:T(8,128)(2,1)}), bf16[1024,1024]{1,0:T(8,128)(2,1)}) %all-gather.15.cloned.1.call-update) | async-done | bytes 2097168 | tf_op jit(solution)/shard_map/all_gather | solution.py:151
  147.1 2.9 copy.89
  150.0 49.2 %all-gather.19.cloned.1.call-done = bf16[1024,1024]{0,1:T(8,128)(2,1)} async-done(((bf16[128,1024]{0,1:T(8,128)(2,1)}), bf16[1024,1024]{0,1:T(8,128)(2,1)}) %all-gather.19.cloned.1.call-update) | async-done | bytes 2097168 | tf_op jit(solution)/shard_map/all_gather | solution.py:150
  199.2 3.4 while.39
  203.7 8.2 while.40
  203.7 2.8 constant_dynamic-slice_fusion.10
  206.7 5.0 fusion.152
  211.9 2.9 convert_element_type.128
  214.8 18.5 %all-gather.23.cloned.1.call-done = bf16[2048,1024]{1,0:T(8,128)(2,1)} async-done(((bf16[512,1024]{1,0:T(8,128)(2,1)}), bf16[2048,1024]{1,0:T(8,128)(2,1)}) %all-gather.23.cloned.1.call-update) | async-done | bytes 4194320 | tf_op jit(solution)/shard_map/all_gather | solution.py:103
  233.3 3.2 multiply_reduce_fusion.8
  237.3 43.9 %all-gather.25.cloned.1.call-done = bf16[1024,3072]{1,0:T(8,128)(2,1)} async-done(((bf16[256,3072]{1,0:T(8,128)(2,1)}), bf16[1024,3072]{1,0:T(8,128)(2,1)}) %all-gather.25.cloned.1.call-update) | async-done | bytes 6291472 | tf_op jit(solution)/shard_map/all_gather | solution.py:104
  281.3 5.0 fusion.80
  286.3 43.0 %all-gather.27.cloned.1.call-done = bf16[1024,3072]{1,0:T(8,128)(2,1)} async-done(((bf16[256,3072]{1,0:T(8,128)(2,1)}), bf16[1024,3072]{1,0:T(8,128)(2,1)}) %all-gather.27.cloned.1.call-update) | async-done | bytes 6291472 | tf_op jit(solution)/shard_map/all_gather | solution.py:105
  329.2 5.1 fusion.81
  334.4 42.8 %all-gather.29.cloned.1.call-done = bf16[3072,1024]{1,0:T(8,128)(2,1)} async-done(((bf16[768,1024]{1,0:T(8,128)(2,1)}), bf16[3072,1024]{1,0:T(8,128)(2,1)}) %all-gather.29.cloned.1.call-update) | async-done | bytes 6291472 | tf_op jit(solution)/shard_map/all_gather | solution.py:106
  377.2 6.6 multiply_convert_fusion
  383.8 5.6 fusion.82
  389.5 2.8 multiply_reduce_fusion.4
  392.6 1.5 convolution_convert_fusion
  395.6 2.5 broadcast_in_dim.47
  398.1 2.5 broadcast_in_dim.47.clone
  400.7 12.9 while.41
  402.9 1.5 fusion.164
  410.2 2.0 copy-done.2
  412.2 1.3 copy-done.4
  413.5 2.5 convert_element_type.143
  416.0 2.6 copy.116
  418.7 2.5 convert_element_type.146
  421.2 2.6 copy.118
  423.9 4.5 fusion.65
  429.6 6.5 fusion.61
  438.4 10.3 fusion.30
  448.8 50.1 %reduce-scatter.16.cloned.1.call-done = bf16[128,1024]{1,0:T(8,128)(2,1)} async-done(((bf16[1024,1024]{1,0:T(8,128)(2,1)}), bf16[128,1024]{1,0:T(8,128)(2,1)}) %reduce-scatter.16.cloned.1.call-update) | async-done | bytes 262160
  500.0 69.9 %reduce-scatter.18.cloned.1.call-done = bf16[128,1024]{1,0:T(8,128)(2,1)} async-done(((bf16[1024,1024]{1,0:T(8,128)(2,1)}), bf16[128,1024]{1,0:T(8,128)(2,1)}) %reduce-scatter.18.cloned.1.call-update) | async-done | bytes 262160
  571.5 10.4 fusion.37
  581.9 29.4 %pad_maximum_fusion = f32[1024,10240]{1,0:T(8,128)} fusion(f32[1024,6144]{1,0:T(8,128)} %fusion.30, f32[1024,4096]{1,0:T(8,128)} %fusion.37), kind=kLoop, calls=%fused_computation.52 | loop fusion | flops 10485760 | bytes 83886080 | tf_op jit(solution)/shard_map/concatenate | solution.py:339
  611.4 31.7 %reduce-scatter.12.cloned.1.call-done = f32[512,1024]{1,0:T(8,128)} async-done(((f32[2048,1024]{1,0:T(8,128)}), f32[512,1024]{1,0:T(8,128)}) %reduce-scatter.12.cloned.1.call-update) | async-done | bytes 2097168 | tf_op jit(solution)/shard_map/reduce_scatter | solution.py:231
  643.1 3.4 copy.122
  646.5 98.5 %reduce-scatter.14.cloned.1.call-done = f32[768,1024]{1,0:T(8,128)} async-done(((f32[3072,1024]{1,0:T(8,128)}), f32[768,1024]{1,0:T(8,128)}) %reduce-scatter.14.cloned.1.call-update) | async-done | bytes 3145744 | tf_op jit(solution)/shard_map/reduce_scatter | solution.py:228
  745.0 4.3 copy.123
  749.3 287.1 %reduce-scatter.10.cloned.1.call-done = f32[256,10240]{1,0:T(8,128)} async-done(((f32[1024,10240]{1,0:T(8,128)}), f32[256,10240]{1,0:T(8,128)}) %reduce-scatter.10.cloned.1.call-update) | async-done | bytes 10485776 | tf_op jit(solution)/shard_map/reduce_scatter | solution.py:338
  1036.4 9.7 copy.121
  1048.0 481.6 %all-reduce.7.cloned.1.call-done = (f32[2621440]{0:T(1024)}, f32[524288]{0:T(1024)}, f32[786432]{0:T(1024)}) async-done(((f32[2621440]{0:T(1024)}, f32[524288]{0:T(1024)}, f32[786432]{0:T(1024)}), (f32[2621440]{0:T(1024)}, f32[524288]{0:T(1024)}, f32[786432]{0:T(1024)})) %all-reduce.7.cloned.1.call-update) | async-done | bytes 15728656
  1529.5 1.7 dynamic-slice.3
  1531.9 1.8 dynamic-slice.5
  1534.6 2.5 dynamic-slice.1
  1537.2 5.1 fusion.36
  1544.6 1.7 fusion.57
  1546.4 40.8 %all-reduce.3 = (f32[1024]{0:T(1024)}, f32[128]{0:T(128)}, f32[128]{0:T(128)}, f32[1024]{0:T(1024)}) all-reduce(f32[1024]{0:T(1024)S(1)} %get-tuple-element.379, f32[128]{0:T(128)S(1)} %get-tuple-element.373, f32[128]{0:T(128)S(1)} %get-tuple-element.377, f32[1024]{0:T(1024)S(1)} %copy-done.55), channel_id=1, replica_groups=mesh['fsdp'=4,'ctx'=8] {'fsdp','ctx'}, use_global_device_ids=true, to_apply=%region_21.22 | all-reduce | flops 2304 | bytes 18432 | tf_op jit(solution)/shard_map/psum | solution.py:347
  1588.2 2.8 reshape.288
  1591.0 51.4 %all-gather.35.cloned.1.call-done = f32[786432]{0:T(1024)} async-done(((f32[98304]{0:T(1024)}), f32[786432]{0:T(1024)}) %all-gather.35.cloned.1.call-update) | async-done | bytes 3145744 | tf_op jit(solution)/shard_map/all_gather | solution.py:77
  1642.3 4.5 reshape.290
  1646.9 147.6 %all-gather.31.cloned.1.call-done = f32[2621440]{0:T(1024)} async-done(((f32[327680]{0:T(1024)}), f32[2621440]{0:T(1024)}) %all-gather.31.cloned.1.call-update) | async-done | bytes 10485776 | tf_op jit(solution)/shard_map/all_gather | solution.py:77
  1794.5 10.6 reshape.286
  1805.0 3.1 slice.60
  1808.2 3.1 fusion.78
  1811.3 6.3 fusion.77
  (236 shorter events, 38.4 us)
Async XLA Ops:
  7.2 30.7 %copy-start.63 = (bf16[128]{0:T(256)(128)(2,1)S(1)}, bf16[128]{0:T(256)(128)(2,1)}, u32[]{:S(2)}) copy-start(bf16[128]{0:T(256)(128)(2,1)} %param.27) | copy-start | bytes 772
  7.2 30.7 %copy-start.61 = (s32[1,128]{1,0:T(1,128)S(1)}, s32[1,128]{1,0:T(1,128)}, u32[]{:S(2)}) copy-start(s32[1,128]{1,0:T(1,128)} %param.21) | copy-start | bytes 1540
  7.2 27.7 %all-gather.13.cloned.1.call-start = ((), (), s32[]{:S(2)}) async-start(), calls=%async_computation.5 | async-start | bytes 2621440 | tf_op jit(solution)/shard_map/all_gather | solution.py:102
  7.9 51.2 %all-gather.17.cloned.1.call-start = ((), (), s32[]{:S(2)}) async-start(), calls=%async_computation.7 | async-start | bytes 2621440 | tf_op jit(solution)/shard_map/all_gather | solution.py:101
  8.7 53.3 %copy-start.11 = (bf16[1,128,1024]{2,1,0:T(8,128)(2,1)S(1)}, bf16[1,128,1024]{2,1,0:T(8,128)(2,1)}, u32[]{:S(2)}) copy-start(bf16[1,128,1024]{2,1,0:T(8,128)(2,1)} %param.20) | copy-start | bytes 786436
  8.7 86.5 %all-gather.21.cloned.1.call-start = ((), (), s32[]{:S(2)}) async-start(), calls=%async_computation.9 | async-start | bytes 5242880 | tf_op jit(solution)/shard_map/all_gather | solution.py:100
  9.4 137.7 %all-gather.15.cloned.1.call-start = ((), (), s32[]{:S(2)}) async-start(), calls=%async_computation.6 | async-start | bytes 2359296 | tf_op jit(solution)/shard_map/all_gather | solution.py:151
  10.2 91.4 %copy-start.45 = (f32[1024]{0:T(1024)}, f32[1024]{0:T(1024)S(1)}, u32[]{:S(2)}) copy-start(f32[1024]{0:T(1024)S(1)} %convert_element_type.118) | copy-start | bytes 12292
  11.8 89.8 %copy-start.51 = (f32[128]{0:T(128)}, f32[128]{0:T(128)S(1)}, u32[]{:S(2)}) copy-start(f32[128]{0:T(128)S(1)} %get-tuple-element.476) | copy-start | bytes 1540
  37.8 161.3 %all-gather.19.cloned.1.call-start = ((), (), s32[]{:S(2)}) async-start(), calls=%async_computation.8 | async-start | bytes 2359296 | tf_op jit(solution)/shard_map/all_gather | solution.py:150
  37.9 25.8 %copy-start.56 = (f32[128]{0:T(128)}, f32[128]{0:T(128)S(1)}, u32[]{:S(2)}) copy-start(f32[128]{0:T(128)S(1)} %convert_element_type.124) | copy-start | bytes 1540
  38.1 67.9 %copy-start.41 = (f32[128,64]{0,1:T(8,128)}, f32[128,64]{0,1:T(8,128)S(1)}, u32[]{:S(2)}) copy-start(f32[128,64]{0,1:T(8,128)S(1)} %get-tuple-element.473) | copy-start | bytes 98308
  38.2 67.9 %copy-start.43 = (f32[128,64]{0,1:T(8,128)}, f32[128,64]{0,1:T(8,128)S(1)}, u32[]{:S(2)}) copy-start(f32[128,64]{0,1:T(8,128)S(1)} %get-tuple-element.474) | copy-start | bytes 98308
  63.6 7.4 copy-start.64
  63.6 7.4 copy-start.60
  64.9 168.4 %all-gather.23.cloned.1.call-start = ((), (), s32[]{:S(2)}) async-start(), calls=%async_computation.10 | async-start | bytes 5242880 | tf_op jit(solution)/shard_map/all_gather | solution.py:103
  65.4 215.8 %all-gather.25.cloned.1.call-start = ((), (), s32[]{:S(2)}) async-start(), calls=%async_computation.11 | async-start | bytes 7864320 | tf_op jit(solution)/shard_map/all_gather | solution.py:104
  66.2 263.0 %all-gather.27.cloned.1.call-start = ((), (), s32[]{:S(2)}) async-start(), calls=%async_computation.12 | async-start | bytes 7864320 | tf_op jit(solution)/shard_map/all_gather | solution.py:105
  66.9 310.3 %all-gather.29.cloned.1.call-start = ((), (), s32[]{:S(2)}) async-start(), calls=%async_computation.13 | async-start | bytes 7864320 | tf_op jit(solution)/shard_map/all_gather | solution.py:106
  67.7 431.1 %reduce-scatter.16.cloned.1.call-start = ((), (), s32[]{:S(2)}) async-start(), calls=%async_computation.20 | async-start | bytes 2359296
  71.0 34.8 %copy-start.58 = (f32[128]{0:T(128)}, f32[128]{0:T(128)S(1)}, u32[]{:S(2)}) copy-start(f32[128]{0:T(128)S(1)} %convert_element_type.127) | copy-start | bytes 1540
  105.8 44.2 %copy-start.47 = (f32[128,16]{0,1:T(8,128)}, f32[128,16]{0,1:T(8,128)S(1)}, u32[]{:S(2)}) copy-start(f32[128,16]{0,1:T(8,128)S(1)} %get-tuple-element.470) | copy-start | bytes 24580
  211.9 74.4 %copy-start.5 = (bf16[1024,1024]{0,1:T(8,128)(2,1)}, bf16[1024,1024]{0,1:T(8,128)(2,1)S(1)}, u32[]{:S(2)}) copy-start(bf16[1024,1024]{0,1:T(8,128)(2,1)S(1)} %get-tuple-element.841) | copy-start | bytes 6291460
  236.4 155.9 %copy-start.16 = (f32[128,1024]{1,0:T(8,128)}, f32[128,1024]{1,0:T(8,128)S(1)}, u32[]{:S(2)}) copy-start(f32[128,1024]{1,0:T(8,128)S(1)} %get-tuple-element.486) | copy-start | bytes 1572868
  329.2 48.0 %copy-start.36 = (f32[128,3072]{1,0:T(8,128)S(1)}, f32[128,3072]{1,0:T(8,128)}, u32[]{:S(2)}) copy-start(f32[128,3072]{1,0:T(8,128)} %fusion.80) | copy-start | bytes 4718596
  329.2 48.0 %copy-start.37 = (bf16[1,128,1024]{2,1,0:T(8,128)(2,1)S(1)}, bf16[1,128,1024]{2,1,0:T(8,128)(2,1)}, u32[]{:S(2)}) copy-start(bf16[1,128,1024]{2,1,0:T(8,128)(2,1)} %param.33) | copy-start | bytes 786436
  383.8 5.6 copy-start.30
  383.8 8.5 copy-start.32
  383.8 5.6 copy-start.10
  389.5 2.9 copy-start.38
  389.5 3.1 copy-start.12
  395.6 5.1 copy-start
  405.1 2.6 copy-start.1
  405.1 3.8 copy-start.3
  410.2 3.3 copy-start.4
  418.6 151.3 %reduce-scatter.18.cloned.1.call-start = ((), (), s32[]{:S(2)}) async-start(), calls=%async_computation.21 | async-start | bytes 2359296
  421.2 2.7 copy-start.24
  421.2 2.7 copy-start.26
  423.8 219.3 %reduce-scatter.12.cloned.1.call-start = ((), (), s32[]{:S(2)}) async-start(), calls=%async_computation.16 | async-start | bytes 10485760 | tf_op jit(solution)/shard_map/reduce_scatter | solution.py:231
  428.4 316.6 %reduce-scatter.14.cloned.1.call-start = ((), (), s32[]{:S(2)}) async-start(), calls=%async_computation.18 | async-start | bytes 15728640 | tf_op jit(solution)/shard_map/reduce_scatter | solution.py:228
  436.1 2.3 copy-start.25
  436.1 600.3 %reduce-scatter.10.cloned.1.call-start = ((), (), s32[]{:S(2)}) async-start(), calls=%async_computation.14 | async-start | bytes 52428800 | tf_op jit(solution)/shard_map/reduce_scatter | solution.py:338
  436.3 2.1 copy-start.31
  438.4 133.1 %copy-start.27 = (bf16[128,16,128]{0,2,1:T(8,128)(2,1)}, bf16[128,16,128]{0,2,1:T(8,128)(2,1)S(1)}, u32[]{:S(2)}) copy-start(bf16[128,16,128]{0,2,1:T(8,128)(2,1)S(1)} %subtract_convert_fusion) | copy-start | bytes 1572868
  438.4 132.7 %copy-start.20 = (f32[128,8,128]{0,2,1:T(8,128)S(1)}, f32[128,8,128]{0,2,1:T(8,128)}, u32[]{:S(2)}) copy-start(f32[128,8,128]{0,2,1:T(8,128)} %copy-done.19) | copy-start | bytes 1572868
  438.4 132.7 %copy-start.50 = (f32[128,8]{0,1:T(8,128)S(1)}, f32[128,8]{0,1:T(8,128)}, u32[]{:S(2)}) copy-start(f32[128,8]{0,1:T(8,128)} %copy-done.49) | copy-start | bytes 12292
  438.4 132.7 %copy-start.57 = (f32[128]{0:T(128)S(1)}, f32[128]{0:T(128)}, u32[]{:S(2)}) copy-start(f32[128]{0:T(128)} %copy-done.56) | copy-start | bytes 1540
  438.4 132.9 %copy-start.54 = (f32[128,8]{0,1:T(8,128)S(1)}, f32[128,8]{0,1:T(8,128)}, u32[]{:S(2)}) copy-start(f32[128,8]{0,1:T(8,128)} %get-tuple-element.471) | copy-start | bytes 12292
  448.8 122.7 %copy-start.46 = (f32[1024]{0:T(1024)S(1)}, f32[1024]{0:T(1024)}, u32[]{:S(2)}) copy-start(f32[1024]{0:T(1024)} %copy-done.45) | copy-start | bytes 12292
  448.8 122.7 %copy-start.52 = (f32[128]{0:T(128)S(1)}, f32[128]{0:T(128)}, u32[]{:S(2)}) copy-start(f32[128]{0:T(128)} %copy-done.51) | copy-start | bytes 1540
  571.5 10.4 copy-start.34
  611.4 918.2 %all-reduce.7.cloned.1.call-start = ((), (), s32[]{:S(2)}) async-start(), calls=%async_computation.22 | async-start | bytes 31457280
  1046.1 491.0 %copy-start.17 = (f32[128,1024]{1,0:T(8,128)S(1)}, f32[128,1024]{1,0:T(8,128)}, u32[]{:S(2)}) copy-start(f32[128,1024]{1,0:T(8,128)} %copy-done.16) | copy-start | bytes 1572868
  1046.1 542.1 %all-gather.33.cloned.1.call-start = ((), (), s32[]{:S(2)}) async-start(), calls=%async_computation.17 | async-start | bytes 2359296 | tf_op jit(solution)/shard_map/all_gather | solution.py:77
  1531.2 111.1 %all-gather.35.cloned.1.call-start = ((), (), s32[]{:S(2)}) async-start(), calls=%async_computation.19 | async-start | bytes 3538944 | tf_op jit(solution)/shard_map/all_gather | solution.py:77
  1533.7 260.7 %all-gather.31.cloned.1.call-start = ((), (), s32[]{:S(2)}) async-start(), calls=%async_computation.15 | async-start | bytes 11796480 | tf_op jit(solution)/shard_map/all_gather | solution.py:77
  1537.1 5.2 copy-start.21
  1537.1 5.2 copy-start.40
  1537.2 6.0 copy-start.22
  1537.2 6.0 copy-start.35
  1542.3 2.2 copy-start.15
  1542.3 2.3 copy-start.28
  1543.2 3.2 copy-start.55
  1543.2 44.0 %copy-start.62 = (f32[128]{0:T(128)S(1)}, f32[128]{0:T(128)}, u32[]{:S(2)}) copy-start(f32[128]{0:T(128)} %get-tuple-element.475) | copy-start | bytes 1540
  (20 other events, 29.0 us)
Sparse Core Ops, SparseCore 0:
  9.6 25.2 all-gather.12
  36.5 22.5 all-gather.16
  60.7 34.4 all-gather.20
  97.7 49.3 all-gather.14
  149.6 49.5 all-gather.18
  200.6 32.6 all-gather.22
  234.8 46.3 all-gather.24
  282.8 46.3 all-gather.26
  330.8 46.3 all-gather.28
  418.8 80.0 reduce-scatter.15
  502.9 66.9 reduce-scatter.17
  572.3 70.7 reduce-scatter.11
  645.9 99.0 reduce-scatter.13
  747.6 288.7 reduce-scatter.9
  1046.3 483.2 all-reduce.6
  1532.1 48.5 all-gather.32
  1583.3 58.9 all-gather.34
  1645.0 149.4 all-gather.30
where the time goes:
time: 1830 us; the launch traced here: 1820 us
  waiting for transfers between devices  1530 us (84%)
  local copies, waits for them, and re-layouts  95.8 us (5%)
  matrix products  88 us (5%)
  other arithmetic  49.4 us (3%)
  blocking collectives  40.8 us (2%)
  between operations  20 us (1%)
    unnamed x21, waiting for transfers between devices  606 us
    reduce_scatter x1, waiting for transfers between devices, local(): lax.psum_scatter(jnp.concatenate([first_part, second_part], axis=1), 'fsd...  287 us
    all_gather x3, waiting for transfers between devices, sum_blocks(): whole_rows = lax.all_gather(pieces, 'ctx', axis=0, tiled=True)  199 us
    reduce_scatter x1, waiting for transfers between devices, local(): lax.psum_scatter(contract_rows(hidden, cotangent), 'fsdp', scatter_dimens...  98.5 us
    all_gather x1, waiting for transfers between devices, local(): lax.all_gather(key_rot, 'ctx', axis=0, tiled=True)  49.2 us
    all_gather x1, waiting for transfers between devices, local(): lax.all_gather(w_gate, 'fsdp', axis=0, tiled=True)  43.9 us
    all_gather x1, waiting for transfers between devices, local(): lax.all_gather(w_up, 'fsdp', axis=0, tiled=True)  43 us
    all_gather x1, waiting for transfers between devices, local(): lax.all_gather(w_down, 'fsdp', axis=0, tiled=True)  42.8 us
  transfers between devices with their start and end apart: 18, of which 17 were waited for; matrix products, arithmetic and copies ran while one was open for 8% of the time, Pallas kernels for 0%

commit v1 on v0

--- a/solution.py
+++ b/solution.py
@@ -364,9 +364,309 @@
     )
 
 
+def split_low(values):
+    high = lax.reduce_precision(values, 8, 7)
+    return high.astype(jnp.bfloat16), (values - high).astype(jnp.bfloat16)
+
+
+def fold_columns(pieces):
+    count, rows, width = pieces.shape
+    half = rows // 2
+    parts = [pieces[:, :, at : at + 1024] for at in range(0, width - 1023, 1024)]
+    if width % 1024:
+        rest = pieces[:, :, width - 512 :]
+        parts.append(jnp.concatenate([rest[:, :half], rest[:, half:]], axis=2))
+    return jnp.concatenate(parts, axis=1) if len(parts) > 1 else parts[0]
+
+
+def unfold_columns(folded, rows, width):
+    parts = [folded[:, at * rows : (at + 1) * rows] for at in range(width // 1024)]
+    if width % 1024:
+        rest = folded[:, (width // 1024) * rows :]
+        parts.append(jnp.concatenate([rest[:, :, :512], rest[:, :, 512:]], axis=1))
+    return jnp.concatenate(parts, axis=2) if len(parts) > 1 else parts[0]
+
+
+def local_by_heads(
+    block_input,
+    positions,
+    attn_norm_gain,
+    w_query,
+    key_projection,
+    value_projection,
+    query_norm_gain,
+    key_norm_gain,
+    output_projection,
+    ffn_norm_gain,
+    w_gate,
+    w_up,
+    w_down,
+    out_cotangent,
+):
+    shards = lax.axis_size("fsdp")
+    blocks = lax.axis_size("ctx")
+    span = block_input.shape[1]
+    width = block_input.shape[2]
+    tokens = shards * span
+    length = blocks * span
+    groups = QUERY_HEADS // KEY_VALUE_HEADS
+    kv_heads = KEY_VALUE_HEADS // shards
+    q_heads = kv_heads * groups
+    q_cols = q_heads * HEAD_SIZE
+    kv_cols = kv_heads * HEAD_SIZE
+    ff_cols = FF // shards
+    scale_factor = 1.0 / math.sqrt(HEAD_SIZE)
+    low = jnp.bfloat16
+    f32 = jnp.float32
+
+    place = positions[0][:, None]
+    codes = jnp.concatenate([place // 32, place % 32], axis=1).astype(low)
+    packed = jnp.concatenate(
+        [block_input[0], out_cotangent[0], jnp.pad(codes, ((0, 0), (0, 126)))], axis=1
+    )
+    packed = lax.all_gather(packed, "fsdp", axis=0, tiled=True)
+    inputs = packed[:, :width].astype(f32)
+    cotangent = packed[:, width : 2 * width]
+    codes = packed[:, 2 * width : 2 * width + 2].astype(jnp.int32)
+    places = codes[:, 0] * 32 + codes[:, 1]
+
+    def by_columns(*matrices):
+        rows = matrices[0].shape[0]
+        cut = jnp.concatenate([m.reshape(rows, shards, -1) for m in matrices], axis=2)
+        cut = jnp.transpose(cut, (1, 0, 2))
+        cut = lax.all_to_all(cut, "fsdp", split_axis=0, concat_axis=0, tiled=True)
+        return cut.reshape(shards * rows, -1)
+
+    attn_weights = by_columns(w_query, key_projection, value_projection)
+    ffn_weights = by_columns(w_gate, w_up)
+
+    gain_one = attn_norm_gain.astype(f32)
+    scale_one = inverse_rms(inputs)
+    normed = (inputs * scale_one * gain_one).astype(low)
+    projected = jnp.dot(normed, attn_weights, preferred_element_type=f32)
+    query = projected[:, :q_cols].reshape(tokens, q_heads, HEAD_SIZE)
+    key = projected[:, q_cols : q_cols + kv_cols].reshape(tokens, kv_heads, HEAD_SIZE)
+    value = projected[:, q_cols + kv_cols :].astype(low)
+    query_scale = inverse_rms(query)
+    key_scale = inverse_rms(key)
+    query_gain = query_norm_gain.astype(f32)
+    key_gain = key_norm_gain.astype(f32)
+    cosine, sine = rope_tables(places)
+    query_rot = apply_rotary(query * query_scale * query_gain, cosine, sine).astype(low)
+    key_rot = apply_rotary(key * key_scale * key_gain, cosine, sine).astype(low)
+    both = jnp.concatenate([key_rot.reshape(tokens, kv_cols), value], axis=1)
+    both = lax.all_gather(both, "ctx", axis=0)
+    both = both.reshape(blocks, shards, span, 2, kv_heads, HEAD_SIZE)
+    both = jnp.transpose(both, (3, 1, 4, 0, 2, 5)).reshape(2, shards, kv_heads, length, HEAD_SIZE)
+    all_keys, all_values = both[0], both[1]
+
+    def per_kv(array):
+        array = array.reshape(shards, span, kv_heads, groups, HEAD_SIZE)
+        return jnp.transpose(array, (0, 2, 3, 1, 4)).reshape(
+            shards, kv_heads, groups * span, HEAD_SIZE
+        )
+
+    def per_token(array):
+        array = array.reshape(shards, kv_heads, groups, span, HEAD_SIZE)
+        return jnp.transpose(array, (0, 3, 1, 2, 4)).reshape(tokens, q_cols)
+
+    query_kv = per_kv(query_rot)
+    row_ids = lax.axis_index("ctx") * span + jnp.arange(span, dtype=jnp.int32)
+    starts = row_ids[None, :] - places.reshape(shards, span)
+    columns = jnp.arange(length, dtype=jnp.int32)
+    allowed = (columns <= row_ids[None, :, None]) & (columns >= starts[:, :, None])
+    allowed = jnp.broadcast_to(
+        allowed[:, None, None], (shards, 1, groups, span, length)
+    ).reshape(shards, 1, groups * span, length)
+    scores = jnp.einsum("skqd,skjd->skqj", query_kv, all_keys, preferred_element_type=f32)
+    scores = jnp.where(allowed, scores * scale_factor, MASK_FLOOR)
+    peak = jnp.max(scores, axis=-1, keepdims=True)
+    log_total = peak + jnp.log(jnp.sum(jnp.exp(scores - peak), axis=-1, keepdims=True))
+    probability = jnp.exp(scores - log_total)
+    probability_low = probability.astype(low)
+    attended = jnp.einsum(
+        "skqj,skjd->skqd", probability_low, all_values, preferred_element_type=f32
+    ).astype(low)
+    attention_output = per_token(attended)
+    partial = jnp.dot(attention_output, output_projection, preferred_element_type=f32)
+    middle = block_input[0].astype(f32) + lax.psum_scatter(
+        partial, "fsdp", scatter_dimension=0, tiled=True
+    )
+    scale_two = inverse_rms(middle)
+    gain_two = ffn_norm_gain.astype(f32)
+    normed_two = lax.all_gather(
+        (middle * scale_two * gain_two).astype(low), "fsdp", axis=0, tiled=True
+    )
+    wide = jnp.dot(normed_two, ffn_weights, preferred_element_type=f32)
+    gate, upper = wide[:, :ff_cols], wide[:, ff_cols:]
+    sigmoid = jax.nn.sigmoid(gate)
+    hidden = (gate * sigmoid * upper).astype(low)
+    down_partial = jnp.dot(hidden, w_down, preferred_element_type=f32)
+    hidden_grad = times_transpose(cotangent, w_down)
+    gate_grad = (hidden_grad * upper * sigmoid * (1.0 + gate * (1.0 - sigmoid))).astype(low)
+    up_grad = (hidden_grad * gate * sigmoid).astype(low)
+    ffn_side = jnp.concatenate([gate_grad, up_grad], axis=1)
+    nt_partial = times_transpose(ffn_side, ffn_weights)
+    pair = jnp.concatenate([down_partial, nt_partial], axis=1).astype(low)
+    pair = lax.psum_scatter(pair, "fsdp", scatter_dimension=0, tiled=True).astype(f32)
+    block_output = (middle + pair[:, :width]).astype(low)[None]
+    nt_grad = pair[:, width:]
+    ffn_gain_term = jnp.sum(nt_grad * middle * scale_two, axis=0)
+    middle_grad = out_cotangent[0].astype(f32) + norm_reverse(
+        nt_grad, middle, scale_two, gain_two
+    )
+    middle_low = lax.all_gather(middle_grad.astype(low), "fsdp", axis=0, tiled=True)
+
+    piece = width // shards // blocks
+
+    def piece_order(array):
+        array = array.reshape(tokens, shards, blocks, piece)
+        return jnp.transpose(array, (0, 2, 1, 3)).reshape(tokens, width)
+
+    def ctx_sum(*pieces):
+        stacked = jnp.concatenate(pieces, axis=1)
+        rows = stacked.shape[1]
+        stacked = stacked.reshape(blocks * rows, width)
+        return lax.psum_scatter(stacked, "ctx", scatter_dimension=0, tiled=True)
+
+    ffn_grads = contract_rows(piece_order(normed_two), ffn_side).astype(low)
+    down_grads = contract_rows(hidden, cotangent).astype(low)
+    ffn_piece = ctx_sum(
+        fold_columns(ffn_grads.reshape(blocks, shards * piece, 2 * ff_cols)),
+        down_grads.reshape(blocks, ff_cols // blocks, width),
+    )
+
+    attn_grad = per_kv(times_transpose(middle_low, output_projection).astype(low))
+    delta = jnp.sum(attn_grad.astype(f32) * attended.astype(f32), axis=-1, keepdims=True)
+    value_part = jnp.einsum(
+        "skqj,skqd->skjd", probability_low, attn_grad, preferred_element_type=f32
+    )
+    prob_grad = jnp.einsum("skqd,skjd->skqj", attn_grad, all_values, preferred_element_type=f32)
+    score_grad = (probability * (prob_grad - delta)).astype(low)
+    query_back = (
+        jnp.einsum("skqj,skjd->skqd", score_grad, all_keys, preferred_element_type=f32)
+        * scale_factor
+    )
+    key_part = (
+        jnp.einsum("skqj,skqd->skjd", score_grad, query_kv, preferred_element_type=f32)
+        * scale_factor
+    )
+    parts = jnp.stack([key_part, value_part]).astype(low)
+    parts = parts.reshape(2, shards, kv_heads, blocks, span, HEAD_SIZE)
+    parts = jnp.transpose(parts, (3, 1, 4, 0, 2, 5)).reshape(blocks * tokens, 2 * kv_cols)
+    sums = lax.psum_scatter(parts, "ctx", scatter_dimension=0, tiled=True).astype(f32)
+    query_pre = reverse_rotary(
+        per_token(query_back).reshape(tokens, q_heads, HEAD_SIZE), cosine, sine
+    )
+    key_pre = reverse_rotary(
+        sums[:, :kv_cols].reshape(tokens, kv_heads, HEAD_SIZE), cosine, sine
+    )
+    query_gain_term = jnp.sum(query_pre * query * query_scale, axis=(0, 1))
+    key_gain_term = jnp.sum(key_pre * key * key_scale, axis=(0, 1))
+    query_low = norm_reverse(query_pre, query, query_scale, query_gain).reshape(tokens, q_cols)
+    key_low = norm_reverse(key_pre, key, key_scale, key_gain).reshape(tokens, kv_cols)
+    attn_side = jnp.concatenate(
+        [query_low.astype(low), key_low.astype(low), sums[:, kv_cols:].astype(low)], axis=1
+    )
+    normed_partial = times_transpose(attn_side, attn_weights)
+    attn_gain_term = jnp.sum(normed_partial * inputs * scale_one, axis=0)
+    normed_grad = lax.psum_scatter(
+        normed_partial.astype(low), "fsdp", scatter_dimension=0, tiled=True
+    ).astype(f32)
+    own = block_input[0].astype(f32)
+    input_grad = middle_grad + norm_reverse(normed_grad, own, inverse_rms(own), gain_one)
+
+    side_cols = q_cols + 2 * kv_cols
+    attn_grads = contract_rows(piece_order(normed), attn_side).astype(low)
+    output_grads = contract_rows(attention_output, middle_low).astype(low)
+    attn_piece = ctx_sum(
+        fold_columns(attn_grads.reshape(blocks, shards * piece, side_cols)),
+        output_grads.reshape(blocks, q_cols // blocks, width),
+    )
+
+    def rows_of(array, rows, cols):
+        return fold_columns(unfold_columns(array[None], rows, cols).reshape(shards, piece, cols))
+
+    ffn_rows = shards * piece * 2 * ff_cols // width
+    attn_rows = shards * piece * side_cols // width
+    gains = jnp.concatenate(
+        [
+            attn_gain_term,
+            ffn_gain_term,
+            query_gain_term,
+            key_gain_term,
+            jnp.zeros((2 * width - 2 * HEAD_SIZE,), f32),
+        ]
+    ).reshape(4, width)
+
+    def gain_rows(values):
+        return jnp.concatenate(split_low(values), axis=-2)
+
+    def gain_values(rows):
+        wide_rows = rows.astype(f32)
+        return wide_rows[..., :4, :] + wide_rows[..., 4:, :]
+
+    outgoing = jnp.concatenate(
+        [
+            rows_of(attn_piece[:attn_rows], shards * piece, side_cols),
+            rows_of(ffn_piece[:ffn_rows], shards * piece, 2 * ff_cols),
+            jnp.broadcast_to(gain_rows(gains)[None], (shards, 8, width)),
+        ],
+        axis=1,
+    )
+    arrived = lax.all_to_all(outgoing, "fsdp", split_axis=0, concat_axis=0, tiled=True)
+    mixed = arrived.shape[1] - 8
+    shard_gains = jnp.sum(gain_values(arrived[:, mixed:]), axis=0)
+    final = jnp.concatenate(
+        [
+            arrived[:, :mixed].reshape(shards * mixed, width),
+            attn_piece[attn_rows:],
+            ffn_piece[ffn_rows:],
+            gain_rows(shard_gains),
+        ],
+        axis=0,
+    )
+    final = lax.all_gather(final, "ctx", axis=0)
+    top = shards * mixed
+    matrices = final[:, :top].reshape(blocks * shards, mixed, width)
+    attn_in = piece * side_cols // width
+    attn_all = unfold_columns(matrices[:, :attn_in], piece, side_cols)
+    ffn_all = unfold_columns(matrices[:, attn_in:], piece, 2 * ff_cols)
+
+    def whole(array, first, last):
+        array = array[:, :, first:last].reshape(blocks, shards, piece, last - first)
+        array = jnp.transpose(array, (0, 2, 1, 3)).astype(f32)
+        return array.reshape(blocks * piece, shards * (last - first))
+
+    out_rows = q_cols // blocks
+    down_rows = ff_cols // blocks
+    output_sum = final[:, top : top + out_rows].reshape(q_cols, width).astype(f32)
+    down_sum = (
+        final[:, top + out_rows : top + out_rows + down_rows].reshape(ff_cols, width).astype(f32)
+    )
+    gain_sums = jnp.sum(gain_values(final[:, top + out_rows + down_rows :]), axis=0)
+    return (
+        block_output,
+        input_grad[None],
+        gain_sums[0],
+        whole(attn_all, 0, q_cols),
+        whole(attn_all, q_cols, q_cols + kv_cols),
+        whole(attn_all, q_cols + kv_cols, side_cols),
+        gain_sums[2, :HEAD_SIZE],
+        gain_sums[2, HEAD_SIZE : 2 * HEAD_SIZE],
+        output_sum,
+        gain_sums[1],
+        whole(ffn_all, 0, ff_cols),
+        whole(ffn_all, ff_cols, 2 * ff_cols),
+        down_sum,
+    )
+
+
 def solution(mesh):
+    shards, blocks = mesh.shape["fsdp"], mesh.shape["ctx"]
+    split_heads = shards == 4 and blocks == 8
     return jax.shard_map(
-        local,
+        local_by_heads if split_heads else local,
         mesh=mesh,
         in_specs=(
             P("fsdp", "ctx", None),

time: 1830 us -> 820 us (0.45)
  waiting for transfers between devices: 1530 us -> 546 us
  blocking collectives: 40.8 us -> 0 us
  matrix products: 88 us -> 52.4 us
  other arithmetic: 49.4 us -> 70.3 us
    unnamed x21 -> x11, waiting for transfers between devices: 606 us -> 0.18 us
    all_gather x12 -> x5, waiting for transfers between devices: 505 us -> 194 us  [the longest x1 120 us: local_by_heads(): final = lax.all_gather(final, 'ctx', axis=0)]
    reduce_scatter x3 -> x6, waiting for transfers between devices: 417 us -> 281 us  [the longest x2 161 us: ctx_sum(): return lax.psum_scatter(stacked, 'ctx', scatter_dimension=0, tiled=True)]
    all_to_all x0 -> x3, waiting for transfers between devices: none -> 70.2 us  [the longest x2 59.4 us: by_columns(): cut = lax.all_to_all(cut, 'fsdp', split_axis=0, concat_axis=0, tiled=True)]
    psum x1 -> x0, blocking collectives: 40.8 us -> none  [local(): lax.psum((attn_gain_term, query_gain_term, key_gain_term, ffn_gain_term),...]
    dot_general x4, matrix products: 31.6 us -> 6.08 us  [contract_rows(): lax.dot_general(left, right, (((0,), (0,)), ((), ())), preferred_element_...]
    concatenate x1 -> x10, other arithmetic: 29.4 us -> 9.84 us  [the longest x2 4.5 us: ctx_sum(): stacked = jnp.concatenate(pieces, axis=1)]
    unnamed x132 -> x131, local copies, waits for them, and re-layouts: 38.7 us -> 31.3 us
  transfers between devices with their start and end apart: 18 -> 14, of which waited for: 17 -> 12; matrix products, arithmetic and copies ran while one was open for 8% -> 12% of each run, Pallas kernels for 0% -> 0%
where the time goes in v1:
time: 820 us; the launch traced here: 812 us
  waiting for transfers between devices  546 us (67%)
  local copies, waits for them, and re-layouts  114 us (14%)
  other arithmetic  70.3 us (9%)
  matrix products  52.4 us (6%)
  between operations  15.5 us (2%)
  starting transfers between devices  14.1 us (2%)
    reduce_scatter x2, waiting for transfers between devices, ctx_sum(): return lax.psum_scatter(stacked, 'ctx', scatter_dimension=0, tiled=True)  161 us
    all_gather x1, waiting for transfers between devices, local_by_heads(): final = lax.all_gather(final, 'ctx', axis=0)  120 us
    all_to_all x2, waiting for transfers between devices, by_columns(): cut = lax.all_to_all(cut, 'fsdp', split_axis=0, concat_axis=0, tiled=True)  59.4 us
    reduce_scatter x1, waiting for transfers between devices, local_by_heads(): lax.psum_scatter(parts, 'ctx', scatter_dimension=0, tiled=True).astype(f32)  58.4 us
    all_gather x1, waiting for transfers between devices, local_by_heads(): both = lax.all_gather(both, 'ctx', axis=0)  57.6 us
    unnamed x131, local copies, waits for them, and re-layouts  31.3 us
    reduce_scatter x1, waiting for transfers between devices, local_by_heads(): lax.psum_scatter(pair, 'fsdp', scatter_dimension=0, tiled=True).astype(f32)  28.9 us
    reduce_scatter x1, waiting for transfers between devices, local_by_heads(): lax.psum_scatter(partial, 'fsdp', scatter_dimension=0, tiled=True)  26.3 us
  transfers between devices with their start and end apart: 14, of which 12 were waited for; matrix products, arithmetic and copies ran while one was open for 12% of the time, Pallas kernels for 0%

profile of v1, /device:TPU:0, one launch (start us, length us, event | category | flops | bytes accessed | tf_op | source)
XLA Modules:
  0.0 812.4 jit_solution(12668096703332867352)
XLA Ops:
  8.2 1.9 fusion.17
  12.8 2.0 copy.184
  14.9 2.5 maximum_bitcast_fusion.2
  17.4 4.6 all-to-all-start
  22.1 35.2 %all-to-all-done = bf16[4,256,1024]{1,2,0:T(8,128)(2,1)} async-done(((bf16[4,256,1024]{1,2,0:T(8,128)(2,1)}), bf16[4,256,1024]{1,2,0:T(8,128)(2,1)}, u32[]{:S(2)}, u32[]{:S(2)}) %all-to-all-start) | async-done | bytes 2097184 | tf_op jit(solution)/shard_map/all_to_all | solution.py:437
  57.3 3.9 copy.185
  61.2 1.7 fusion.2
  76.1 2.3 slice.265
  81.2 1.7 copy.186
  85.7 1.7 multiply_multiply_fusion
  91.1 57.6 %all-gather.14.cloned.1.call-done = bf16[4096,512]{1,0:T(8,128)(2,1)} async-done(((bf16[512,512]{1,0:T(8,128)(2,1)}), bf16[4096,512]{1,0:T(8,128)(2,1)}) %all-gather.14.cloned.1.call-update) | async-done | bytes 4194320 | tf_op jit(solution)/shard_map/all_gather | solution.py:458
  148.7 6.9 reshape.582
  155.7 4.8 fusion.48
  163.0 2.0 fusion.1
  165.0 2.5 exponential_reduce_fusion
  168.2 3.0 convolution_convert_fusion.7
  173.4 2.0 reshape.584
  175.5 3.4 fusion.54
  178.9 2.6 copy.195
  181.5 2.7 copy.196
  184.2 4.1 maximum_bitcast_fusion.1
  188.4 5.2 all-to-all-start.1
  193.6 26.3 %reduce-scatter.7.cloned.1.call-done = f32[128,1024]{1,0:T(8,128)} async-done(((f32[512,1024]{1,0:T(8,128)}), f32[128,1024]{1,0:T(8,128)}) %reduce-scatter.7.cloned.1.call-update) | async-done | bytes 524304 | tf_op jit(solution)/shard_map/reduce_scatter | solution.py:492
  222.9 24.2 %all-to-all-done.1 = bf16[4,256,1536]{1,2,0:T(8,128)(2,1)} async-done(((bf16[4,256,1536]{1,2,0:T(8,128)(2,1)}), bf16[4,256,1536]{1,2,0:T(8,128)(2,1)}, u32[]{:S(2)}, u32[]{:S(2)}) %all-to-all-start.1) | async-done | bytes 3145760 | tf_op jit(solution)/shard_map/all_to_all | solution.py:437
  247.0 4.6 copy.197
  251.7 4.0 fusion.55
  255.7 2.8 multiply_convert_fusion.3
  261.3 1.8 convolution_convert_fusion.5
  264.7 28.9 %reduce-scatter.9.cloned.1.call-done = bf16[128,2048]{1,0:T(8,128)(2,1)} async-done(((bf16[512,2048]{1,0:T(8,128)(2,1)}), bf16[128,2048]{1,0:T(8,128)(2,1)}) %reduce-scatter.9.cloned.1.call-update) | async-done | bytes 524304 | tf_op jit(solution)/shard_map/reduce_scatter | solution.py:511
  295.0 2.1 fusion.45
  297.2 16.8 %all-gather.12.cloned.1.call-done = bf16[512,1024]{1,0:T(8,128)(2,1)} async-done(((bf16[128,1024]{1,0:T(8,128)(2,1)}), bf16[512,1024]{1,0:T(8,128)(2,1)}) %all-gather.12.cloned.1.call-update) | async-done | bytes 1048592 | tf_op jit(solution)/shard_map/all_gather | solution.py:518
  314.0 3.1 convolution_convert_fusion.8
  317.1 2.1 reshape.588
  320.9 7.7 convolution_convert_fusion.1
  328.6 6.4 multiply_convert_fusion
  337.1 2.2 copy.205
  339.3 3.5 copy.206
  342.8 9.5 %maximum_bitcast_fusion = bf16[8,4,128,2,2,128]{5,4,3,2,1,0:T(2,128)(2,1)} fusion(bf16[1,4,2,8,128,128]{5,2,0,4,1,3:T(2,128)(2,1)} %copy.206, bf16[1,4,2,8,128,128]{5,2,0,4,1,3:T(2,128)(2,1)S(1)} %copy.205), kind=kLoop, calls=%fused_computation.7 | loop fusion | flops 2097152 | bytes 8388608 | tf_op jit(solution)/shard_map/transpose | solution.py:556
  352.3 7.2 reshape.591
  362.4 1.8 convolution_convert_fusion
  365.6 2.3 convolution_convert_fusion.3
  368.0 2.4 pad_maximum_fusion
  371.6 1.7 copy.210
  375.1 2.3 copy.211
  377.4 4.2 convolution_multiply_fusion
  389.1 58.4 %reduce-scatter.11.cloned.1.call-done = bf16[512,512]{1,0:T(8,128)(2,1)} async-done(((bf16[4096,512]{1,0:T(8,128)(2,1)}), bf16[512,512]{1,0:T(8,128)(2,1)}) %reduce-scatter.11.cloned.1.call-update) | async-done | bytes 524304 | tf_op jit(solution)/shard_map/reduce_scatter | solution.py:557
  447.5 1.8 slice_convert_fusion.1
  456.4 2.1 pad_maximum_fusion.1
  458.6 88.2 %reduce-scatter.17.cloned.1.call-done = bf16[288,1024]{1,0:T(8,128)(2,1)} async-done(((bf16[2304,1024]{1,0:T(8,128)(2,1)}), bf16[288,1024]{1,0:T(8,128)(2,1)}) %reduce-scatter.17.cloned.1.call-update) | async-done | bytes 589840 | tf_op jit(solution)/shard_map/reduce_scatter | solution.py:530
  548.0 4.2 fusion.6
  552.3 73.2 %reduce-scatter.15.cloned.1.call-done = bf16[192,1024]{1,0:T(8,128)(2,1)} async-done(((bf16[1536,1024]{1,0:T(8,128)(2,1)}), bf16[192,1024]{1,0:T(8,128)(2,1)}) %reduce-scatter.15.cloned.1.call-update) | async-done | bytes 393232 | tf_op jit(solution)/shard_map/reduce_scatter | solution.py:530
  627.4 3.6 all-to-all-start.2
  631.1 10.9 %all-to-all-done.2 = bf16[4,88,1024]{2,1,0:T(8,128)(2,1)S(1)} async-done(((bf16[4,88,1024]{2,1,0:T(8,128)(2,1)}), bf16[4,88,1024]{2,1,0:T(8,128)(2,1)S(1)}, u32[]{:S(2)}, u32[]{:S(2)}) %all-to-all-start.2) | async-done | bytes 720928 | tf_op jit(solution)/shard_map/all_to_all | solution.py:617
  642.1 4.2 concatenate.112
  646.3 6.3 reduce-scatter.13.cloned.1.call-done
  653.8 2.0 fusion.22
  655.8 119.6 %all-gather.16.cloned.1.call-done = bf16[3904,1024]{1,0:T(8,128)(2,1)} async-done(((bf16[488,1024]{1,0:T(8,128)(2,1)}), bf16[3904,1024]{1,0:T(8,128)(2,1)}) %all-gather.16.cloned.1.call-update) | async-done | bytes 7995408 | tf_op jit(solution)/shard_map/all_gather | solution.py:629
  775.4 3.5 slice.306
  785.2 2.0 copy.218
  787.2 2.2 copy.234
  789.8 2.0 copy.217
  791.9 2.2 copy.233
  795.7 2.2 copy.230
  801.9 2.2 bitcast_convert_fusion
  (277 shorter events, 83.9 us)
Async XLA Ops:
  7.2 248.5 %copy-start = (bf16[768,1024]{1,0:T(8,128)(2,1)S(1)}, bf16[768,1024]{1,0:T(8,128)(2,1)}, u32[]{:S(2)}) copy-start(bf16[768,1024]{1,0:T(8,128)(2,1)} %param.26) | copy-start | bytes 4718596
  7.2 54.0 %all-gather.8.cloned.1.call-start = ((), (), s32[]{:S(2)}) async-start(), calls=%async_computation.9 | async-start | bytes 2785280 | tf_op jit(solution)/shard_map/all_gather | solution.py:427
  17.3 4.7 copy-start.45
  17.3 4.7 copy-start.48
  17.4 39.9 %all-to-all-start = ((bf16[4,256,1024]{1,2,0:T(8,128)(2,1)}), bf16[4,256,1024]{1,2,0:T(8,128)(2,1)}, u32[]{:S(2)}, u32[]{:S(2)}) async-start(bf16[4,256,1024]{1,2,0:T(8,128)(2,1)} %maximum_bitcast_fusion.2), calls=%async_computation | async-start | bytes 4194304 | tf_op jit(solution)/shard_map/all_to_all | solution.py:437
  22.0 126.7 %all-gather.14.cloned.1.call-start = ((), (), s32[]{:S(2)}) async-start(), calls=%async_computation.18 | async-start | bytes 4718592 | tf_op jit(solution)/shard_map/all_gather | solution.py:458
  22.1 48.2 %copy-start.41 = (f32[128]{0:T(128)}, f32[128]{0:T(128)S(1)}, u32[]{:S(2)}) copy-start(f32[128]{0:T(128)S(1)} %convert_element_type.183) | copy-start | bytes 1540
  61.2 3.2 copy-start.27
  62.9 1.6 copy-start.38
  64.5 1.3 copy-start.18
  65.8 1.3 copy-start.15
  68.3 5.2 copy-start.22
  72.7 2.7 copy-start.49
  75.2 144.8 %reduce-scatter.7.cloned.1.call-start = ((), (), s32[]{:S(2)}) async-start(), calls=%async_computation.10 | async-start | bytes 2621440 | tf_op jit(solution)/shard_map/reduce_scatter | solution.py:492
  75.9 4.0 copy-start.43
  85.7 1.7 copy-start.9
  88.3 1.4 copy-start.12
  88.3 1.6 copy-start.44
  161.0 1.8 copy-start.3
  161.0 1.4 copy-start.25
  161.0 1.9 copy-start.13
  161.6 5.9 copy-start.28
  162.8 4.7 copy-start.4
  164.9 3.3 copy-start.2
  188.4 5.2 copy-start.46
  188.4 58.7 %all-to-all-start.1 = ((bf16[4,256,1536]{1,2,0:T(8,128)(2,1)}), bf16[4,256,1536]{1,2,0:T(8,128)(2,1)}, u32[]{:S(2)}, u32[]{:S(2)}) async-start(bf16[4,256,1536]{1,2,0:T(8,128)(2,1)} %maximum_bitcast_fusion.1), calls=%async_computation.2 | async-start | bytes 6291456 | tf_op jit(solution)/shard_map/all_to_all | solution.py:437
  193.6 58.1 %all-gather.10.cloned.1.call-start = ((), (), s32[]{:S(2)}) async-start(), calls=%async_computation.11 | async-start | bytes 1310720 | tf_op jit(solution)/shard_map/all_gather | solution.py:497
  222.8 70.8 %reduce-scatter.9.cloned.1.call-start = ((), (), s32[]{:S(2)}) async-start(), calls=%async_computation.12 | async-start | bytes 2621440 | tf_op jit(solution)/shard_map/reduce_scatter | solution.py:511
  258.5 1.4 copy-start.54
  258.6 2.7 copy-start.21
  264.6 30.2 %copy-start.7 = (f32[128,1024]{1,0:T(8,128)S(1)}, f32[128,1024]{1,0:T(8,128)}, u32[]{:S(2)}) copy-start(f32[128,1024]{1,0:T(8,128)} %copy-done.6) | copy-start | bytes 1572868
  264.6 49.4 %all-gather.12.cloned.1.call-start = ((), (), s32[]{:S(2)}) async-start(), calls=%async_computation.13 | async-start | bytes 1310720 | tf_op jit(solution)/shard_map/all_gather | solution.py:518
  297.1 23.3 %copy-start.32 = (bf16[4,2,256,128]{3,2,1,0:T(8,128)(2,1)S(1)}, bf16[4,2,256,128]{3,2,1,0:T(8,128)(2,1)}, u32[]{:S(2)}) copy-start(bf16[4,2,256,128]{3,2,1,0:T(8,128)(2,1)} %copy-done.31) | copy-start | bytes 1572868
  297.1 150.4 %reduce-scatter.11.cloned.1.call-start = ((), (), s32[]{:S(2)}) async-start(), calls=%async_computation.14 | async-start | bytes 4718592 | tf_op jit(solution)/shard_map/reduce_scatter | solution.py:557
  317.1 3.8 copy-start.5
  319.1 9.4 %slice-start = ((s8[8388608]{0:T(1024)(128)(4,1)}), s8[4194304]{0:T(1024)(128)(4,1)S(1)}, s32[]{:S(2)}) async-start(s8[8388608]{0:T(1024)(128)(4,1)} %bitcast.235), calls=%async_computation.20 | async-start | bytes 8388608
  320.8 7.7 slice-start.1
  328.6 6.4 copy-start.14
  335.0 2.1 copy-start.20
  337.1 2.2 copy-start.29
  359.5 187.3 %reduce-scatter.17.cloned.1.call-start = ((), (), s32[]{:S(2)}) async-start(), calls=%async_computation.17 | async-start | bytes 5308416 | tf_op jit(solution)/shard_map/reduce_scatter | solution.py:530
  361.1 1.4 copy-start.55
  364.5 1.1 copy-start.51
  370.4 1.3 copy-start.19
  370.4 255.1 %reduce-scatter.15.cloned.1.call-start = ((), (), s32[]{:S(2)}) async-start(), calls=%async_computation.16 | async-start | bytes 3538944 | tf_op jit(solution)/shard_map/reduce_scatter | solution.py:530
  383.6 1.4 copy-start.26
  383.6 1.4 copy-start.47
  385.0 1.4 copy-start.24
  385.0 2.0 copy-start.34
  385.8 1.8 copy-start.16
  450.6 2.0 copy-start.23
  450.6 2.6 copy-start.33
  452.6 2.5 copy-start.35
  452.6 2.5 copy-start.36
  452.7 2.5 copy-start.37
  458.5 89.5 %copy-start.39 = (f32[512]{0:T(512)S(1)}, f32[512]{0:T(512)}, u32[]{:S(2)}) copy-start(f32[512]{0:T(512)} %copy-done.38) | copy-start | bytes 6148
  458.5 194.1 %reduce-scatter.13.cloned.1.call-start = ((), (), s32[]{:S(2)}) async-start(), calls=%async_computation.15 | async-start | bytes 1310720 | tf_op jit(solution)/shard_map/reduce_scatter | solution.py:573
  627.4 14.7 %slice-start.2 = ((bf16[288,1024]{1,0:T(8,128)(2,1)}), bf16[96,1024]{1,0:T(8,128)(2,1)S(1)}, s32[]{:S(2)}) async-start(bf16[288,1024]{1,0:T(8,128)(2,1)} %reduce-scatter.17.cloned.1.call-done), calls=%async_computation.22 | async-start | bytes 393216 | tf_op jit(solution)/shard_map/slice | solution.py:624
  627.4 14.7 %slice-start.3 = ((bf16[192,1024]{1,0:T(8,128)(2,1)}), bf16[64,1024]{1,0:T(8,128)(2,1)S(1)}, s32[]{:S(2)}) async-start(bf16[192,1024]{1,0:T(8,128)(2,1)} %reduce-scatter.15.cloned.1.call-done), calls=%async_computation.23 | async-start | bytes 262144 | tf_op jit(solution)/shard_map/slice | solution.py:623
  627.4 14.5 %all-to-all-start.2 = ((bf16[4,88,1024]{2,1,0:T(8,128)(2,1)}), bf16[4,88,1024]{2,1,0:T(8,128)(2,1)S(1)}, u32[]{:S(2)}, u32[]{:S(2)}) async-start(bf16[4,88,1024]{2,1,0:T(8,128)(2,1)} %pad_maximum_fusion.10), calls=%async_computation.8 | async-start | bytes 1441792 | tf_op jit(solution)/shard_map/all_to_all | solution.py:617
  631.0 144.4 %all-gather.16.cloned.1.call-start = ((), (), s32[]{:S(2)}) async-start(), calls=%async_computation.19 | async-start | bytes 8994816 | tf_op jit(solution)/shard_map/all_gather | solution.py:629
  631.1 21.5 %copy-start.17 = (bf16[1,128,1024]{2,1,0:T(8,128)(2,1)S(1)}, bf16[1,128,1024]{2,1,0:T(8,128)(2,1)}, u32[]{:S(2)}) copy-start(bf16[1,128,1024]{2,1,0:T(8,128)(2,1)} %param.14) | copy-start | bytes 786436
  642.0 11.8 %copy-start.30 = (f32[128,1024]{1,0:T(8,128)S(1)}, f32[128,1024]{1,0:T(8,128)}, u32[]{:S(2)}) copy-start(f32[128,1024]{1,0:T(8,128)} %get-tuple-element.22) | copy-start | bytes 1572868
  801.9 3.8 copy-start.1
  (10 other events, 8.6 us)
Sparse Core Ops, SparseCore 0:
  10.2 34.8 all-gather.7
  75.3 73.3 all-gather.13
  179.0 40.8 reduce-scatter.6
  222.9 22.6 all-gather.9
  264.8 28.8 reduce-scatter.8
  297.2 16.7 all-gather.11
  359.6 87.8 reduce-scatter.10
  451.6 95.1 reduce-scatter.16
  551.4 74.0 reduce-scatter.14
  628.6 23.9 reduce-scatter.12
  655.4 119.9 all-gather.15
